TPU v7x, 128 devices: a whole 4x4x4 slice. The times are simulated.
128 devices in a mesh: dp: 8 (over x, core), vocab: 16 (over y, z).
Axes of the slice: x: 4, y: 4, z: 4, core: 2. Of those that a mesh axis runs over, the one named last changes fastest.
Arguments:
- hidden_rows: bfloat16 [5120, 2048], P(('dp', 'vocab')), parts along dimension 0, may hold values from -10 to 10
- head_weight: bfloat16 [2048, 77824], P(None, 'vocab'), may hold values from -0.15 to 1
Outputs:
- token_probs: bfloat16 [5120, 77824], P('dp', 'vocab'), parts along dimension 0
There are 8 independent parts, one for each index of `dp`. A program takes and returns all parts, laid end to end along the dimension named above; an argument that names none is the same for every part. Nothing has to cross between parts.
All inputs are finite; a program needn't handle non-finite values.
Results may differ from a plain program's by a relative error of at most 0.012.
Values may be sent and summed in bfloat16 or wider, within the bound.
A program may use at most 128 MiB of HBM per device.

v0:
```python
import jax
import jax.numpy as jnp
from jax import lax
from jax.sharding import PartitionSpec as P


def body(hidden_rows, head_weight):
    gathered = lax.all_gather(hidden_rows, "vocab", axis=0, tiled=True)
    logits = jnp.dot(gathered, head_weight, preferred_element_type=jnp.float32)
    local_peak = jnp.max(logits, axis=1)
    peak = lax.pmax(local_peak, "vocab")
    ratio = jnp.exp(logits - peak[:, None])
    kept = ratio * jnp.clip((ratio - 0.05) / 0.05, 0.0, 1.0)
    local_mass = jnp.sum(kept, axis=1)
    mass = lax.psum(local_mass, "vocab")
    return (kept / mass[:, None]).astype(jnp.bfloat16)


def solution(mesh):
    in_specs = (P(("dp", "vocab"), None), P(None, "vocab"))
    out_specs = P("dp", "vocab")
    return jax.shard_map(body, mesh=mesh, in_specs=in_specs, out_specs=out_specs, check_vma=False)
```

profile of v0, /device:TPU:0, one launch (start us, length us, event | category | flops | bytes accessed | tf_op | source)
XLA Modules:
  0.0 177.8 jit_solution(6624829475127733169)
XLA Ops:
  6.5 0.0 all-gather.2.cloned.1.call-start
  6.5 0.7 all-gather.2.cloned.1.call-update
  7.3 51.2 %all-gather.2.cloned.1.call-done = bf16[640,2048]{1,0:T(8,128)(2,1)} async-done(((bf16[40,2048]{1,0:T(8,128)(2,1)}), bf16[640,2048]{1,0:T(8,128)(2,1)}) %all-gather.2.cloned.1.call-update) | async-done | bytes 2621456 | tf_op jit(solution)/shard_map/all_gather | solution.py:8
  58.5 21.1 %fusion.1 = (f32[640]{0:T(1024)S(1)}, f32[640,4864]{1,0:T(8,128)}) fusion(bf16[640,2048]{1,0:T(8,128)(2,1)} %all-gather.2.cloned.1.call-done, bf16[2048,4864]{1,0:T(8,128)(2,1)} %param.3), kind=kOutput, calls=%fused_computation.3 | convolution fusion | flops 12753796096 | bytes 34998784 | tf_op jit(solution)/shard_map/dot_general | solution.py:9
  79.6 38.2 %pmax.7 = f32[640]{0:T(1024)S(1)} all-reduce(f32[640]{0:T(1024)S(1)} %get-tuple-element.5), channel_id=1, replica_groups=mesh['dp'=8,'vocab'=16] {'vocab'}, use_global_device_ids=true, to_apply=%region_1.0 | all-reduce | flops 640 | bytes 5120 | tf_op jit(solution)/shard_map/pmax | solution.py:11
  117.7 7.9 %fusion = f32[640]{0:T(1024)S(1)} fusion(f32[640,4864]{1,0:T(8,128)} %get-tuple-element.6, f32[640]{0:T(1024)S(1)} %pmax.7), kind=kLoop, calls=%fused_computation.2 | loop fusion | flops 18677120 | bytes 12456960 | tf_op jit(solution)/shard_map/reduce_sum | solution.py:14
  125.6 35.5 %psum.7 = f32[640]{0:T(1024)S(1)} all-reduce(f32[640]{0:T(1024)S(1)} %fusion), channel_id=1, replica_groups=mesh['dp'=8,'vocab'=16] {'vocab'}, use_global_device_ids=true, to_apply=%region_3.4 | all-reduce | flops 640 | bytes 5120 | tf_op jit(solution)/shard_map/psum | solution.py:15
  161.1 9.8 %divide_convert_fusion = bf16[640,4864]{1,0:T(8,128)(2,1)} fusion(f32[640,4864]{1,0:T(8,128)} %get-tuple-element.6, f32[640]{0:T(1024)S(1)} %psum.7, f32[640]{0:T(1024)S(1)} %pmax.7), kind=kLoop, calls=%fused_computation | loop fusion | flops 21790720 | bytes 18682880 | tf_op jit(solution)/shard_map/convert_element_type | solution.py:16
Async XLA Ops:
  6.5 51.9 %all-gather.2.cloned.1.call-start = ((), (), s32[]{:S(2)}) async-start(), calls=%async_computation | async-start | bytes 2785280 | tf_op jit(solution)/shard_map/all_gather | solution.py:8
Sparse Core Ops, SparseCore 0:
  9.5 48.8 all-gather.1
where the time goes:
time: 178 us
  blocking collectives  73.6 us (41%)
  waiting for transfers between devices  51.9 us (29%)
  matrix products  21.1 us (12%)
  other arithmetic  17.7 us (10%)
  between operations  13.4 us (8%)
    all_gather x1, waiting for transfers between devices, body(): gathered = lax.all_gather(hidden_rows, 'vocab', axis=0, tiled=True)  51.2 us
    pmax x1, blocking collectives, body(): peak = lax.pmax(local_peak, 'vocab')  38.2 us
    psum x1, blocking collectives, body(): mass = lax.psum(local_mass, 'vocab')  35.5 us
    dot_general x1, matrix products, body(): logits = jnp.dot(gathered, head_weight, preferred_element_type=jnp.float32)  21.1 us
    convert_element_type x1, other arithmetic, body(): return (kept / mass[:, None]).astype(jnp.bfloat16)  9.84 us
    reduce_sum x1, other arithmetic, body(): local_mass = jnp.sum(kept, axis=1)  7.88 us
  transfers between devices with their start and end apart: 1, of which 1 were waited for; matrix products, arithmetic and copies ran while one was open for 0% of the time, Pallas kernels for 0%

commit v1 on v0

v1 whole, which is shorter than its diff:
```python
import jax
import jax.numpy as jnp
from jax import lax
from jax.experimental import pallas as pl
from jax.experimental.pallas import tpu as pltpu
from jax.sharding import PartitionSpec as P

MESH = pl.DeviceIdType.MESH
F32 = jnp.float32
BLOCK = 40
HALF = 1024
GROUPS = (
    ((0, 0), (3, 0), (1, 0), (0, 1)),
    ((0, 3), (2, 0), (3, 1), (3, 3)),
    ((1, 1), (1, 3), (2, 1), (2, 3)),
    ((0, 2), (3, 2), (1, 2), (2, 2)),
)
ARRIVALS = (
    (3, 0, "w"), (1, 0, "w"), (2, 0, 0), (2, 0, 1),
    (0, 3, "w"), (0, 1, "w"), (3, 3, "w"), (3, 1, "w"), (1, 3, "w"), (1, 1, "w"), (2, 3, "w"), (2, 1, "w"),
    (0, 2, "w"), (3, 2, "w"), (1, 2, 0), (1, 2, 1), (2, 2, 0), (2, 2, 1),
)


def to_row(tile):
    return jnp.transpose(tile)


def to_column(row):
    return jnp.transpose(jnp.broadcast_to(row, (128, 128)))


def kernel(x_hbm, w_hbm, kept, scale, w, xb, xs, lane, peak_col, row_send, row_recv,
           w_sem, own_sem, send_sem, recv_sem, row_send_sem, row_recv_sem):
    core = lax.rem(lax.axis_index("dp"), 2)
    me = lax.axis_index("vocab")
    y, z = me // 4, lax.rem(me, 4)
    a, b = z + core * (y - z), y + core * (z - y)
    stride_a, stride_b = 1 + 3 * core, 4 - 3 * core

    def block(da, db):
        return lax.rem(a + da, 4) * stride_a + lax.rem(b + db, 4) * stride_b

    def rows_of(da, db):
        return pl.ds(pl.multiple_of(block(da, db) * BLOCK, 8), BLOCK)

    w_copy = pltpu.make_async_copy(w_hbm, w, w_sem)
    w_copy.start()
    own_copy = pltpu.make_async_copy(x_hbm, xb.at[me], own_sem)
    own_copy.start()

    barrier = pltpu.get_barrier_semaphore()
    neighbours = (block(1, 0), block(3, 0), block(0, 1), block(0, 3))
    for peer in neighbours:
        pl.semaphore_signal(barrier, inc=1, device_id={"vocab": peer}, device_id_type=MESH)
    pl.semaphore_wait(barrier, 4)

    started = []

    def part(ref, half):
        return ref if half == "w" else ref.at[:, pl.ds(half * HALF, HALF)]

    def send(da, db, half, to):
        ta, tb = to
        slot = ARRIVALS.index(((da - ta) % 4, (db - tb) % 4, half))
        here = x_hbm if (da, db) == (0, 0) else xb.at[block(da, db)]
        copy = pltpu.make_async_remote_copy(
            src_ref=part(here, half),
            dst_ref=part(xb.at[block(da, db)], half),
            send_sem=send_sem.at[slot],
            recv_sem=recv_sem.at[slot],
            device_id={"vocab": block(ta, tb)},
            device_id_type=MESH,
        )
        copy.start()
        started.append(copy)

    def arrive(da, db, half):
        slot = ARRIVALS.index((da, db, half))
        ref = part(xb.at[block(da, db)], half)
        pltpu.make_async_copy(ref, ref, recv_sem.at[slot]).wait()

    A_UP, A_DOWN, B_UP, B_DOWN = (1, 0), (3, 0), (0, 1), (0, 3)

    def multiply(group, columns):
        at = [rows_of(*g) for g in group]
        first = columns[0] == 0
        best = None if first else [lane[r, :] for r in at]
        for c in range(columns[0], columns[1], 256):
            out = jnp.dot(xs[...], w[:, c:c + 256], preferred_element_type=F32)
            for i, r in enumerate(at):
                piece = out[i * BLOCK:(i + 1) * BLOCK]
                kept[r, c:c + 256] = piece
                top = jnp.maximum(piece[:, :128], piece[:, 128:])
                if best is None or len(best) <= i:
                    best = (best or []) + [top]
                else:
                    best[i] = jnp.maximum(best[i], top)
        for i, r in enumerate(at):
            lane[r, :] = best[i]

    def gather_group(group):
        xs[...] = jnp.concatenate([xb[block(*g)] for g in group], axis=0)

    send(0, 0, "w", A_UP)
    send(0, 0, "w", A_DOWN)
    send(0, 0, "w", B_UP)
    send(0, 0, "w", B_DOWN)
    own_copy.wait()
    arrive(3, 0, "w")
    send(3, 0, 0, A_UP)
    send(3, 0, "w", B_UP)
    send(3, 0, "w", B_DOWN)
    arrive(1, 0, "w")
    send(1, 0, 1, A_DOWN)
    send(1, 0, "w", B_UP)
    send(1, 0, "w", B_DOWN)
    arrive(0, 3, "w")
    send(0, 3, "w", B_UP)
    arrive(0, 1, "w")
    w_copy.wait()
    gather_group(GROUPS[0])
    multiply(GROUPS[0], (0, 2304))
    arrive(2, 0, 0)
    arrive(2, 0, 1)
    send(2, 0, "w", B_UP)
    send(2, 0, "w", B_DOWN)
    multiply(GROUPS[0], (2304, 4864))
    arrive(3, 3, "w")
    arrive(3, 1, "w")
    send(3, 1, "w", B_DOWN)
    gather_group(GROUPS[1])
    multiply(GROUPS[1], (0, 2304))
    arrive(1, 3, "w")
    send(1, 3, 0, B_UP)
    arrive(1, 1, "w")
    send(1, 1, 1, B_DOWN)
    multiply(GROUPS[1], (2304, 4864))
    arrive(2, 3, "w")
    send(2, 3, 0, B_UP)
    arrive(2, 1, "w")
    send(2, 1, 1, B_DOWN)
    gather_group(GROUPS[2])
    multiply(GROUPS[2], (0, 4864))
    for last in ARRIVALS[12:]:
        arrive(*last)
    gather_group(GROUPS[3])
    multiply(GROUPS[3], (0, 4864))

    def exchange(step):
        for i in range(1, 16):
            copy = pltpu.make_async_remote_copy(
                src_ref=row_send.at[step],
                dst_ref=row_recv.at[step, 15 - i],
                send_sem=row_send_sem.at[step],
                recv_sem=row_recv_sem.at[step],
                device_id={"vocab": lax.rem(me + i, 16)},
                device_id_type=MESH,
            )
            copy.start()

    def exchanged(step):
        pltpu.make_async_copy(row_recv.at[step], row_recv.at[step], row_recv_sem.at[step]).wait()

    tiles = [slice(i * 128, (i + 1) * 128) for i in range(5)]
    for t in tiles:
        row_send[0, :, t] = jnp.max(to_row(lane[t, :]), axis=0, keepdims=True)
    exchange(0)
    for t in tiles:
        peak_col[t, :] = to_column(row_send[0, :, t])

    @pl.loop(0, 40)
    def _(i):
        r = pl.ds(pl.multiple_of(i * 16, 16), 16)
        top = peak_col[r, :]
        for c in range(0, 4864, 128):
            kept[r, c:c + 128] = jnp.exp(kept[r, c:c + 128] - top)

    exchanged(0)
    local = row_send[0]
    peak = jnp.maximum(local, jnp.max(row_recv[0], axis=0))
    shrink = jnp.exp(local - peak)
    for t in tiles:
        peak_col[t, :] = to_column(shrink[:, t] * 20.0)

    @pl.loop(0, 40)
    def _(i):
        r = pl.ds(pl.multiple_of(i * 16, 16), 16)
        factor = peak_col[r, :]
        total = jnp.zeros((16, 128), F32)
        for c in range(0, 4864, 128):
            ratio = kept[r, c:c + 128]
            value = ratio * jnp.clip(ratio * factor - 1.0, 0.0, 1.0)
            kept[r, c:c + 128] = value
            total = total + value
        lane[r, :] = total

    for t in tiles:
        row_send[1, :, t] = jnp.sum(to_row(lane[t, :]), axis=0, keepdims=True) * shrink[:, t]
    exchange(1)
    exchanged(1)
    mass = row_send[1] + jnp.sum(row_recv[1], axis=0)
    final = shrink / mass
    for t in tiles:
        scale[t, :] = to_column(final[:, t])

    for copy in started:
        copy.wait_send()
    for step in range(2):
        pltpu.make_async_copy(row_recv.at[step], row_recv.at[step], row_send_sem.at[step]).wait()


def finish(kept, scale, out, stage, sem):
    copies = []
    for i in range(10):
        @pl.loop(0, 4)
        def _(j):
            r = pl.ds(pl.multiple_of(i * 64 + j * 16, 16), 16)
            factor = scale[r, :]
            for c in range(0, 4864, 128):
                stage[r, c:c + 128] = (kept[r, c:c + 128] * factor).astype(jnp.bfloat16)
        rows = pl.ds(i * 64, 64)
        copy = pltpu.make_async_copy(stage.at[rows, :], out.at[rows, :], sem.at[i])
        copy.start()
        copies.append(copy)
    for copy in copies:
        copy.wait()


def body(hidden_rows, head_weight):
    kept, scale = pl.pallas_call(
        kernel,
        out_shape=(pltpu.VMEM((640, 4864), F32), pltpu.VMEM((640, 128), F32)),
        in_specs=[pl.BlockSpec(memory_space=pl.ANY)] * 2,
        out_specs=(pl.BlockSpec(memory_space=pltpu.VMEM),) * 2,
        scratch_shapes=[
            pltpu.VMEM((2048, 4864), jnp.bfloat16),
            pltpu.VMEM((16, BLOCK, 2048), jnp.bfloat16),
            pltpu.VMEM((4 * BLOCK, 2048), jnp.bfloat16),
            pltpu.VMEM((640, 128), F32),
            pltpu.VMEM((640, 128), F32),
            pltpu.VMEM((2, 1, 640), F32),
            pltpu.VMEM((2, 15, 1, 640), F32),
            pltpu.SemaphoreType.DMA,
            pltpu.SemaphoreType.DMA,
            pltpu.SemaphoreType.DMA((18,)),
            pltpu.SemaphoreType.DMA((18,)),
            pltpu.SemaphoreType.DMA((2,)),
            pltpu.SemaphoreType.DMA((2,)),
        ],
        compiler_params=pltpu.CompilerParams(
            collective_id=0, has_side_effects=True, vmem_limit_bytes=32 * 2**20
        ),
        cost_estimate=pl.CostEstimate(flops=2 * 640 * 2048 * 4864, bytes_accessed=36 * 10**6, transcendentals=640 * 4864),
    )(hidden_rows, head_weight)
    kept = pltpu.with_memory_space_constraint(kept, pltpu.VMEM)
    scale = pltpu.with_memory_space_constraint(scale, pltpu.VMEM)
    return pl.pallas_call(
        finish,
        out_shape=jax.ShapeDtypeStruct((640, 4864), jnp.bfloat16),
        in_specs=[pl.BlockSpec(memory_space=pltpu.VMEM)] * 2,
        out_specs=pl.BlockSpec(memory_space=pl.ANY),
        scratch_shapes=[pltpu.VMEM((640, 4864), jnp.bfloat16), pltpu.SemaphoreType.DMA((10,))],
        compiler_params=pltpu.CompilerParams(vmem_limit_bytes=10 * 2**20),
        cost_estimate=pl.CostEstimate(flops=640 * 4864, bytes_accessed=19 * 10**6, transcendentals=0),
    )(kept, scale)


def solution(mesh):
    in_specs = (P(("dp", "vocab"), None), P(None, "vocab"))
    out_specs = P("dp", "vocab")
    return jax.shard_map(body, mesh=mesh, in_specs=in_specs, out_specs=out_specs, check_vma=False)
```

time: 178 us -> 45.3 us (0.25)
  blocking collectives: 73.6 us -> 0 us
  waiting for transfers between devices: 51.9 us -> 0 us
  Pallas kernels: 0 us -> 44.3 us
  matrix products: 21.1 us -> 0 us
  other arithmetic: 17.7 us -> 0 us
  between operations: 13.4 us -> 0.01 us
    all_gather x1 -> x0, waiting for transfers between devices: 51.2 us -> none  [body(): gathered = lax.all_gather(hidden_rows, 'vocab', axis=0, tiled=True)]
    pallas_call x0 -> x2, Pallas kernels: none -> 44.3 us  [the longest x1 41.5 us: body(): pl.pallas_call(kernel, out_shape=(pltpu.VMEM((640, 4864), F32), pltpu.VME...]
    pmax x1 -> x0, blocking collectives: 38.2 us -> none  [body(): peak = lax.pmax(local_peak, 'vocab')]
    psum x1 -> x0, blocking collectives: 35.5 us -> none  [body(): mass = lax.psum(local_mass, 'vocab')]
    dot_general x1 -> x0, matrix products: 21.1 us -> none  [body(): logits = jnp.dot(gathered, head_weight, preferred_element_type=jnp.float32)]
    convert_element_type x1 -> x0, other arithmetic: 9.84 us -> none  [body(): return (kept / mass[:, None]).astype(jnp.bfloat16)]
    reduce_sum x1 -> x0, other arithmetic: 7.88 us -> none  [body(): local_mass = jnp.sum(kept, axis=1)]
  transfers between devices with their start and end apart: 1 -> 0, of which waited for: 1 -> 0; matrix products, arithmetic and copies ran while one was open for 0% -> 0% of each run, Pallas kernels for 0% -> 0%
where the time goes in v1:
time: 45.3 us; the launch traced here: 45.2 us
  Pallas kernels  44.3 us (98%)
  local copies, waits for them, and re-layouts  0.92 us (2%)
    pallas_call x1, Pallas kernels, body(): pl.pallas_call(kernel, out_shape=(pltpu.VMEM((640, 4864), F32), pltpu.VME...  41.5 us
    pallas_call x1, Pallas kernels, body(): pl.pallas_call(finish, out_shape=jax.ShapeDtypeStruct((640, 4864), jnp.bf...  2.84 us
    unnamed x2, local copies, waits for them, and re-layouts  0.92 us

profile of v1, /device:TPU:0, one launch (start us, length us, event | category | flops | bytes accessed | tf_op | source)
XLA Modules:
  0.0 45.2 jit_solution(6022175098345889878)
XLA Ops:
  0.0 0.0 copy-start
  0.0 0.9 %copy-done = bf16[40,2048]{1,0:T(8,128)(2,1)S(1)} copy-done((bf16[40,2048]{1,0:T(8,128)(2,1)S(1)}, bf16[40,2048]{1,0:T(8,128)(2,1)}, u32[]{:S(2)}) %copy-start) | copy-done | bytes 163864
  0.9 41.5 %shard_map.28 = (f32[640,4864]{1,0:T(8,128)S(1)}, f32[640,128]{1,0:T(8,128)S(1)}) custom-call(bf16[40,2048]{1,0:T(8,128)(2,1)S(1)} %copy-done, bf16[2048,4864]{1,0:T(8,128)(2,1)} %w_hbm.1), custom_call_target="tpu_custom_call" | custom-call | flops 12750684160 | bytes 36000000 | tf_op jit(solution)/shard_map/pallas_call | solution.py:231
  42.4 2.8 %shard_map.29 = bf16[640,4864]{1,0:T(8,128)(2,1)} custom-call(f32[640,4864]{1,0:T(8,128)S(1)} %get-tuple-element.7.kept, f32[640,128]{1,0:T(8,128)S(1)} %get-tuple-element.8.scale), custom_call_target="tpu_custom_call" | custom-call | flops 3112960 | bytes 19000000 | tf_op jit(solution)/shard_map/pallas_call | solution.py:258
Async XLA Ops:
  0.0 0.9 %copy-start = (bf16[40,2048]{1,0:T(8,128)(2,1)S(1)}, bf16[40,2048]{1,0:T(8,128)(2,1)}, u32[]{:S(2)}) copy-start(bf16[40,2048]{1,0:T(8,128)(2,1)} %x_hbm.1) | copy-start | bytes 491524

commit v2 on v1

--- a/solution.py
+++ b/solution.py
@@ -10,16 +10,17 @@
 BLOCK = 40
 HALF = 1024
 GROUPS = (
-    ((0, 0), (3, 0), (1, 0), (0, 1)),
-    ((0, 3), (2, 0), (3, 1), (3, 3)),
-    ((1, 1), (1, 3), (2, 1), (2, 3)),
-    ((0, 2), (3, 2), (1, 2), (2, 2)),
+    ((0, 0), (3, 0), (1, 0)),
+    ((2, 0), (0, 3), (0, 1)),
+    ((3, 3), (3, 1), (1, 3), (1, 1)),
+    ((2, 3), (2, 1), (0, 2)),
+    ((3, 2), (1, 2), (2, 2)),
 )
-ARRIVALS = (
-    (3, 0, "w"), (1, 0, "w"), (2, 0, 0), (2, 0, 1),
-    (0, 3, "w"), (0, 1, "w"), (3, 3, "w"), (3, 1, "w"), (1, 3, "w"), (1, 1, "w"), (2, 3, "w"), (2, 1, "w"),
-    (0, 2, "w"), (3, 2, "w"), (1, 2, 0), (1, 2, 1), (2, 2, 0), (2, 2, 1),
-)
+ARRIVALS = tuple((da, db, half) for da in range(4) for db in range(4) for half in (0, 1) if (da, db) != (0, 0))
+PEERS = tuple(sorted(
+    ((da, db) for da in range(4) for db in range(4) if (da, db) != (0, 0)),
+    key=lambda p: -(min(p[0], 4 - p[0]) + min(p[1], 4 - p[1])),
+))
 
 
 def to_row(tile):
@@ -58,27 +59,28 @@
     started = []
 
     def part(ref, half):
-        return ref if half == "w" else ref.at[:, pl.ds(half * HALF, HALF)]
-
-    def send(da, db, half, to):
-        ta, tb = to
-        slot = ARRIVALS.index(((da - ta) % 4, (db - tb) % 4, half))
-        here = x_hbm if (da, db) == (0, 0) else xb.at[block(da, db)]
-        copy = pltpu.make_async_remote_copy(
-            src_ref=part(here, half),
-            dst_ref=part(xb.at[block(da, db)], half),
-            send_sem=send_sem.at[slot],
-            recv_sem=recv_sem.at[slot],
-            device_id={"vocab": block(ta, tb)},
-            device_id_type=MESH,
-        )
-        copy.start()
-        started.append(copy)
-
-    def arrive(da, db, half):
-        slot = ARRIVALS.index((da, db, half))
-        ref = part(xb.at[block(da, db)], half)
-        pltpu.make_async_copy(ref, ref, recv_sem.at[slot]).wait()
+        return ref.at[:, pl.ds(half * HALF, HALF)]
+
+    def send(da, db, half, *directions):
+        for ta, tb in directions:
+            slot = ARRIVALS.index(((da - ta) % 4, (db - tb) % 4, half))
+            ref = part(xb.at[block(da, db)], half)
+            copy = pltpu.make_async_remote_copy(
+                src_ref=ref,
+                dst_ref=ref,
+                send_sem=send_sem.at[slot],
+                recv_sem=recv_sem.at[slot],
+                device_id={"vocab": block(ta, tb)},
+                device_id_type=MESH,
+            )
+            copy.start()
+            started.append(copy)
+
+    def arrive(da, db, *halves):
+        for half in halves:
+            slot = ARRIVALS.index((da, db, half))
+            ref = part(xb.at[block(da, db)], half)
+            pltpu.make_async_copy(ref, ref, recv_sem.at[slot]).wait()
 
     A_UP, A_DOWN, B_UP, B_DOWN = (1, 0), (3, 0), (0, 1), (0, 3)
 
@@ -87,7 +89,7 @@
         first = columns[0] == 0
         best = None if first else [lane[r, :] for r in at]
         for c in range(columns[0], columns[1], 256):
-            out = jnp.dot(xs[...], w[:, c:c + 256], preferred_element_type=F32)
+            out = jnp.dot(xs[:len(group) * BLOCK, :], w[:, c:c + 256], preferred_element_type=F32)
             for i, r in enumerate(at):
                 piece = out[i * BLOCK:(i + 1) * BLOCK]
                 kept[r, c:c + 256] = piece
@@ -100,61 +102,82 @@
             lane[r, :] = best[i]
 
     def gather_group(group):
-        xs[...] = jnp.concatenate([xb[block(*g)] for g in group], axis=0)
-
-    send(0, 0, "w", A_UP)
-    send(0, 0, "w", A_DOWN)
-    send(0, 0, "w", B_UP)
-    send(0, 0, "w", B_DOWN)
+        xs[:len(group) * BLOCK, :] = jnp.concatenate([xb[block(*g)] for g in group], axis=0)
+
     own_copy.wait()
-    arrive(3, 0, "w")
+    send(0, 0, 0, A_UP)
+    send(0, 0, 1, A_DOWN)
+    send(0, 0, 1, A_UP)
+    send(0, 0, 0, A_DOWN)
+    send(0, 0, 0, B_UP)
+    send(0, 0, 1, B_DOWN)
+    send(0, 0, 1, B_UP)
+    send(0, 0, 0, B_DOWN)
+    arrive(3, 0, 0)
     send(3, 0, 0, A_UP)
-    send(3, 0, "w", B_UP)
-    send(3, 0, "w", B_DOWN)
-    arrive(1, 0, "w")
+    arrive(1, 0, 1)
     send(1, 0, 1, A_DOWN)
-    send(1, 0, "w", B_UP)
-    send(1, 0, "w", B_DOWN)
-    arrive(0, 3, "w")
-    send(0, 3, "w", B_UP)
-    arrive(0, 1, "w")
+    send(3, 0, 0, B_UP, B_DOWN)
+    send(1, 0, 1, B_UP, B_DOWN)
+    arrive(3, 0, 1)
+    send(3, 0, 1, B_UP, B_DOWN)
+    arrive(1, 0, 0)
+    send(1, 0, 0, B_UP, B_DOWN)
+    arrive(0, 3, 0)
+    send(0, 3, 0, B_UP)
+    arrive(0, 1, 1)
+    send(0, 1, 1, B_DOWN)
     w_copy.wait()
     gather_group(GROUPS[0])
     multiply(GROUPS[0], (0, 2304))
     arrive(2, 0, 0)
+    send(2, 0, 0, B_UP, B_DOWN)
     arrive(2, 0, 1)
-    send(2, 0, "w", B_UP)
-    send(2, 0, "w", B_DOWN)
+    send(2, 0, 1, B_UP, B_DOWN)
     multiply(GROUPS[0], (2304, 4864))
-    arrive(3, 3, "w")
-    arrive(3, 1, "w")
-    send(3, 1, "w", B_DOWN)
+    arrive(0, 3, 1)
+    arrive(0, 1, 0)
     gather_group(GROUPS[1])
     multiply(GROUPS[1], (0, 2304))
-    arrive(1, 3, "w")
+    arrive(3, 3, 0)
+    send(3, 3, 0, B_UP)
+    arrive(3, 1, 1)
+    send(3, 1, 1, B_DOWN)
+    multiply(GROUPS[1], (2304, 4864))
+    arrive(1, 3, 0)
     send(1, 3, 0, B_UP)
-    arrive(1, 1, "w")
+    arrive(1, 1, 1)
     send(1, 1, 1, B_DOWN)
-    multiply(GROUPS[1], (2304, 4864))
-    arrive(2, 3, "w")
+    arrive(3, 3, 1)
+    arrive(3, 1, 0)
+    arrive(1, 3, 1)
+    arrive(1, 1, 0)
+    gather_group(GROUPS[2])
+    multiply(GROUPS[2], (0, 2304))
+    arrive(2, 3, 0)
     send(2, 3, 0, B_UP)
-    arrive(2, 1, "w")
+    arrive(2, 1, 1)
     send(2, 1, 1, B_DOWN)
-    gather_group(GROUPS[2])
-    multiply(GROUPS[2], (0, 4864))
-    for last in ARRIVALS[12:]:
-        arrive(*last)
+    multiply(GROUPS[2], (2304, 4864))
+    arrive(2, 3, 1)
+    arrive(2, 1, 0)
+    arrive(0, 2, 0, 1)
     gather_group(GROUPS[3])
     multiply(GROUPS[3], (0, 4864))
+    arrive(3, 2, 0, 1)
+    arrive(1, 2, 0, 1)
+    arrive(2, 2, 0, 1)
+    gather_group(GROUPS[4])
+    multiply(GROUPS[4], (0, 4864))
 
     def exchange(step):
-        for i in range(1, 16):
+        for i, peer in enumerate(PEERS):
             copy = pltpu.make_async_remote_copy(
                 src_ref=row_send.at[step],
-                dst_ref=row_recv.at[step, 15 - i],
+                dst_ref=row_recv.at[step, i],
                 send_sem=row_send_sem.at[step],
                 recv_sem=row_recv_sem.at[step],
-                device_id={"vocab": lax.rem(me + i, 16)},
+                device_id={"vocab": block(*peer)},
                 device_id_type=MESH,
             )
             copy.start()
@@ -169,9 +192,9 @@
     for t in tiles:
         peak_col[t, :] = to_column(row_send[0, :, t])
 
-    @pl.loop(0, 40)
+    @pl.loop(0, 20)
     def _(i):
-        r = pl.ds(pl.multiple_of(i * 16, 16), 16)
+        r = pl.ds(pl.multiple_of(i * 32, 32), 32)
         top = peak_col[r, :]
         for c in range(0, 4864, 128):
             kept[r, c:c + 128] = jnp.exp(kept[r, c:c + 128] - top)
@@ -183,11 +206,11 @@
     for t in tiles:
         peak_col[t, :] = to_column(shrink[:, t] * 20.0)
 
-    @pl.loop(0, 40)
+    @pl.loop(0, 20)
     def _(i):
-        r = pl.ds(pl.multiple_of(i * 16, 16), 16)
+        r = pl.ds(pl.multiple_of(i * 32, 32), 32)
         factor = peak_col[r, :]
-        total = jnp.zeros((16, 128), F32)
+        total = jnp.zeros((32, 128), F32)
         for c in range(0, 4864, 128):
             ratio = kept[r, c:c + 128]
             value = ratio * jnp.clip(ratio * factor - 1.0, 0.0, 1.0)
@@ -212,14 +235,14 @@
 
 def finish(kept, scale, out, stage, sem):
     copies = []
-    for i in range(10):
-        @pl.loop(0, 4)
+    for i in range(20):
+        @pl.loop(0, 2)
         def _(j):
-            r = pl.ds(pl.multiple_of(i * 64 + j * 16, 16), 16)
+            r = pl.ds(pl.multiple_of(i * 32 + j * 16, 16), 16)
             factor = scale[r, :]
             for c in range(0, 4864, 128):
                 stage[r, c:c + 128] = (kept[r, c:c + 128] * factor).astype(jnp.bfloat16)
-        rows = pl.ds(i * 64, 64)
+        rows = pl.ds(i * 32, 32)
         copy = pltpu.make_async_copy(stage.at[rows, :], out.at[rows, :], sem.at[i])
         copy.start()
         copies.append(copy)
@@ -228,10 +251,11 @@
 
 
 def body(hidden_rows, head_weight):
+    hidden_rows = pltpu.with_memory_space_constraint(hidden_rows, pltpu.HBM)
     kept, scale = pl.pallas_call(
         kernel,
         out_shape=(pltpu.VMEM((640, 4864), F32), pltpu.VMEM((640, 128), F32)),
-        in_specs=[pl.BlockSpec(memory_space=pl.ANY)] * 2,
+        in_specs=[pl.BlockSpec(memory_space=pltpu.HBM)] * 2,
         out_specs=(pl.BlockSpec(memory_space=pltpu.VMEM),) * 2,
         scratch_shapes=[
             pltpu.VMEM((2048, 4864), jnp.bfloat16),
@@ -243,8 +267,8 @@
             pltpu.VMEM((2, 15, 1, 640), F32),
             pltpu.SemaphoreType.DMA,
             pltpu.SemaphoreType.DMA,
-            pltpu.SemaphoreType.DMA((18,)),
-            pltpu.SemaphoreType.DMA((18,)),
+            pltpu.SemaphoreType.DMA((30,)),
+            pltpu.SemaphoreType.DMA((30,)),
             pltpu.SemaphoreType.DMA((2,)),
             pltpu.SemaphoreType.DMA((2,)),
         ],
@@ -260,7 +284,7 @@
         out_shape=jax.ShapeDtypeStruct((640, 4864), jnp.bfloat16),
         in_specs=[pl.BlockSpec(memory_space=pltpu.VMEM)] * 2,
         out_specs=pl.BlockSpec(memory_space=pl.ANY),
-        scratch_shapes=[pltpu.VMEM((640, 4864), jnp.bfloat16), pltpu.SemaphoreType.DMA((10,))],
+        scratch_shapes=[pltpu.VMEM((640, 4864), jnp.bfloat16), pltpu.SemaphoreType.DMA((20,))],
         compiler_params=pltpu.CompilerParams(vmem_limit_bytes=10 * 2**20),
         cost_estimate=pl.CostEstimate(flops=640 * 4864, bytes_accessed=19 * 10**6, transcendentals=0),
     )(kept, scale)

time: 45.3 us -> 49.8 us (1.099)
  Pallas kernels: 44.3 us -> 49.5 us
  local copies, waits for them, and re-layouts: 0.92 us -> 0 us
    pallas_call x1, Pallas kernels: 41.5 us -> 46.7 us  [body(): pl.pallas_call(kernel, out_shape=(pltpu.VMEM((640, 4864), F32), pltpu.VME...]
    unnamed x2 -> x0, local copies, waits for them, and re-layouts: 0.92 us -> none
where the time goes in v2:
time: 49.8 us; the launch traced here: 49.7 us
  Pallas kernels  49.5 us (99%)
    pallas_call x1, Pallas kernels, body(): pl.pallas_call(kernel, out_shape=(pltpu.VMEM((640, 4864), F32), pltpu.VME...  46.7 us
    pallas_call x1, Pallas kernels, body(): pl.pallas_call(finish, out_shape=jax.ShapeDtypeStruct((640, 4864), jnp.bf...  2.85 us

profile of v2, /device:TPU:0, one launch (start us, length us, event | category | flops | bytes accessed | tf_op | source)
XLA Modules:
  0.0 49.7 jit_solution(8528294911283015867)
XLA Ops:
  0.0 46.7 %shard_map.28 = (f32[640,4864]{1,0:T(8,128)S(1)}, f32[640,128]{1,0:T(8,128)S(1)}) custom-call(bf16[40,2048]{1,0:T(8,128)(2,1)} %x_hbm.1, bf16[2048,4864]{1,0:T(8,128)(2,1)} %w_hbm.1), custom_call_target="tpu_custom_call" | custom-call | flops 12750684160 | bytes 36000000 | tf_op jit(solution)/shard_map/pallas_call | solution.py:255
  46.7 2.9 %shard_map.29 = bf16[640,4864]{1,0:T(8,128)(2,1)} custom-call(f32[640,4864]{1,0:T(8,128)S(1)} %get-tuple-element.7.kept, f32[640,128]{1,0:T(8,128)S(1)} %get-tuple-element.8.scale), custom_call_target="tpu_custom_call" | custom-call | flops 3112960 | bytes 19000000 | tf_op jit(solution)/shard_map/pallas_call | solution.py:282

commit v3 on v2

--- a/solution.py
+++ b/solution.py
@@ -10,11 +10,11 @@
 BLOCK = 40
 HALF = 1024
 GROUPS = (
-    ((0, 0), (3, 0), (1, 0)),
-    ((2, 0), (0, 3), (0, 1)),
-    ((3, 3), (3, 1), (1, 3), (1, 1)),
-    ((2, 3), (2, 1), (0, 2)),
-    ((3, 2), (1, 2), (2, 2)),
+    ((0, 0),),
+    ((3, 0), (1, 0), (0, 3), (0, 1)),
+    ((2, 0), (3, 3), (3, 1)),
+    ((1, 3), (1, 1), (2, 3), (2, 1)),
+    ((0, 2), (3, 2), (1, 2), (2, 2)),
 )
 ARRIVALS = tuple((da, db, half) for da in range(4) for db in range(4) for half in (0, 1) if (da, db) != (0, 0))
 PEERS = tuple(sorted(
@@ -23,6 +23,10 @@
 ))
 
 
+def size_of(group):
+    return max(len(group) * BLOCK, 128)
+
+
 def to_row(tile):
     return jnp.transpose(tile)
 
@@ -31,7 +35,7 @@
     return jnp.transpose(jnp.broadcast_to(row, (128, 128)))
 
 
-def kernel(x_hbm, w_hbm, kept, scale, w, xb, xs, lane, peak_col, row_send, row_recv,
+def kernel(x_hbm, w_hbm, kept, scale, w, xb, xs, square, lane, peak_col, row_send, row_recv,
            w_sem, own_sem, send_sem, recv_sem, row_send_sem, row_recv_sem):
     core = lax.rem(lax.axis_index("dp"), 2)
     me = lax.axis_index("vocab")
@@ -45,10 +49,15 @@
     def rows_of(da, db):
         return pl.ds(pl.multiple_of(block(da, db) * BLOCK, 8), BLOCK)
 
-    w_copy = pltpu.make_async_copy(w_hbm, w, w_sem)
-    w_copy.start()
+    def load(i):
+        depth = pl.ds(i % 2 * 1024, 1024)
+        columns = pl.ds(0, 2304) if i < 2 else pl.ds(2304, 2560)
+        return pltpu.make_async_copy(w_hbm.at[depth, columns], w.at[depth, columns], w_sem.at[i])
+
     own_copy = pltpu.make_async_copy(x_hbm, xb.at[me], own_sem)
     own_copy.start()
+    for i in range(4):
+        load(i).start(priority=1)
 
     barrier = pltpu.get_barrier_semaphore()
     neighbours = (block(1, 0), block(3, 0), block(0, 1), block(0, 3))
@@ -89,7 +98,7 @@
         first = columns[0] == 0
         best = None if first else [lane[r, :] for r in at]
         for c in range(columns[0], columns[1], 256):
-            out = jnp.dot(xs[:len(group) * BLOCK, :], w[:, c:c + 256], preferred_element_type=F32)
+            out = jnp.dot(xs[:size_of(group), :], w[:, c:c + 256], preferred_element_type=F32)
             for i, r in enumerate(at):
                 piece = out[i * BLOCK:(i + 1) * BLOCK]
                 kept[r, c:c + 256] = piece
@@ -102,7 +111,10 @@
             lane[r, :] = best[i]
 
     def gather_group(group):
-        xs[:len(group) * BLOCK, :] = jnp.concatenate([xb[block(*g)] for g in group], axis=0)
+        pieces = [xb[block(*g)] for g in group]
+        if len(group) * BLOCK < 128:
+            pieces.append(jnp.zeros((128 - len(group) * BLOCK, 2048), jnp.bfloat16))
+        xs[:size_of(group), :] = jnp.concatenate(pieces, axis=0)
 
     own_copy.wait()
     send(0, 0, 0, A_UP)
@@ -113,12 +125,19 @@
     send(0, 0, 1, B_DOWN)
     send(0, 0, 1, B_UP)
     send(0, 0, 0, B_DOWN)
+    gather_group(GROUPS[0])
+    load(0).wait()
+    load(1).wait()
+    multiply(GROUPS[0], (0, 2304))
     arrive(3, 0, 0)
     send(3, 0, 0, A_UP)
     arrive(1, 0, 1)
     send(1, 0, 1, A_DOWN)
     send(3, 0, 0, B_UP, B_DOWN)
     send(1, 0, 1, B_UP, B_DOWN)
+    load(2).wait()
+    load(3).wait()
+    multiply(GROUPS[0], (2304, 4864))
     arrive(3, 0, 1)
     send(3, 0, 1, B_UP, B_DOWN)
     arrive(1, 0, 0)
@@ -127,46 +146,40 @@
     send(0, 3, 0, B_UP)
     arrive(0, 1, 1)
     send(0, 1, 1, B_DOWN)
-    w_copy.wait()
-    gather_group(GROUPS[0])
-    multiply(GROUPS[0], (0, 2304))
+    arrive(0, 3, 1)
+    arrive(0, 1, 0)
+    gather_group(GROUPS[1])
+    multiply(GROUPS[1], (0, 2304))
     arrive(2, 0, 0)
     send(2, 0, 0, B_UP, B_DOWN)
     arrive(2, 0, 1)
     send(2, 0, 1, B_UP, B_DOWN)
-    multiply(GROUPS[0], (2304, 4864))
-    arrive(0, 3, 1)
-    arrive(0, 1, 0)
-    gather_group(GROUPS[1])
-    multiply(GROUPS[1], (0, 2304))
+    multiply(GROUPS[1], (2304, 4864))
     arrive(3, 3, 0)
     send(3, 3, 0, B_UP)
     arrive(3, 1, 1)
     send(3, 1, 1, B_DOWN)
-    multiply(GROUPS[1], (2304, 4864))
+    arrive(3, 3, 1)
+    arrive(3, 1, 0)
+    gather_group(GROUPS[2])
+    multiply(GROUPS[2], (0, 2304))
     arrive(1, 3, 0)
     send(1, 3, 0, B_UP)
     arrive(1, 1, 1)
     send(1, 1, 1, B_DOWN)
-    arrive(3, 3, 1)
-    arrive(3, 1, 0)
-    arrive(1, 3, 1)
-    arrive(1, 1, 0)
-    gather_group(GROUPS[2])
-    multiply(GROUPS[2], (0, 2304))
+    multiply(GROUPS[2], (2304, 4864))
     arrive(2, 3, 0)
     send(2, 3, 0, B_UP)
     arrive(2, 1, 1)
     send(2, 1, 1, B_DOWN)
-    multiply(GROUPS[2], (2304, 4864))
+    arrive(1, 3, 1)
+    arrive(1, 1, 0)
     arrive(2, 3, 1)
     arrive(2, 1, 0)
-    arrive(0, 2, 0, 1)
     gather_group(GROUPS[3])
     multiply(GROUPS[3], (0, 4864))
-    arrive(3, 2, 0, 1)
-    arrive(1, 2, 0, 1)
-    arrive(2, 2, 0, 1)
+    for last in GROUPS[4]:
+        arrive(*last, 0, 1)
     gather_group(GROUPS[4])
     multiply(GROUPS[4], (0, 4864))
 
@@ -197,7 +210,9 @@
         r = pl.ds(pl.multiple_of(i * 32, 32), 32)
         top = peak_col[r, :]
         for c in range(0, 4864, 128):
-            kept[r, c:c + 128] = jnp.exp(kept[r, c:c + 128] - top)
+            ratio = jnp.exp(kept[r, c:c + 128] - top)
+            kept[r, c:c + 128] = ratio
+            square[r, c:c + 128] = ratio * ratio
 
     exchanged(0)
     local = row_send[0]
@@ -213,7 +228,7 @@
         total = jnp.zeros((32, 128), F32)
         for c in range(0, 4864, 128):
             ratio = kept[r, c:c + 128]
-            value = ratio * jnp.clip(ratio * factor - 1.0, 0.0, 1.0)
+            value = jnp.minimum(jnp.maximum(square[r, c:c + 128] * factor - ratio, 0.0), ratio)
             kept[r, c:c + 128] = value
             total = total + value
         lane[r, :] = total
@@ -261,11 +276,12 @@
             pltpu.VMEM((2048, 4864), jnp.bfloat16),
             pltpu.VMEM((16, BLOCK, 2048), jnp.bfloat16),
             pltpu.VMEM((4 * BLOCK, 2048), jnp.bfloat16),
+            pltpu.VMEM((640, 4864), F32),
             pltpu.VMEM((640, 128), F32),
             pltpu.VMEM((640, 128), F32),
             pltpu.VMEM((2, 1, 640), F32),
             pltpu.VMEM((2, 15, 1, 640), F32),
-            pltpu.SemaphoreType.DMA,
+            pltpu.SemaphoreType.DMA((4,)),
             pltpu.SemaphoreType.DMA,
             pltpu.SemaphoreType.DMA((30,)),
             pltpu.SemaphoreType.DMA((30,)),
@@ -273,7 +289,7 @@
             pltpu.SemaphoreType.DMA((2,)),
         ],
         compiler_params=pltpu.CompilerParams(
-            collective_id=0, has_side_effects=True, vmem_limit_bytes=32 * 2**20
+            collective_id=0, has_side_effects=True, vmem_limit_bytes=42 * 2**20
         ),
         cost_estimate=pl.CostEstimate(flops=2 * 640 * 2048 * 4864, bytes_accessed=36 * 10**6, transcendentals=640 * 4864),
     )(hidden_rows, head_weight)

time: 49.8 us -> 42.8 us (0.86)
  Pallas kernels: 49.5 us -> 42.5 us
    pallas_call x1, Pallas kernels: 46.7 us -> 39.6 us  [body(): pl.pallas_call(kernel, out_shape=(pltpu.VMEM((640, 4864), F32), pltpu.VME...]
where the time goes in v3:
time: 42.8 us; the launch traced here: 42.7 us
  Pallas kernels  42.5 us (99%)
    pallas_call x1, Pallas kernels, body(): pl.pallas_call(kernel, out_shape=(pltpu.VMEM((640, 4864), F32), pltpu.VME...  39.6 us
    pallas_call x1, Pallas kernels, body(): pl.pallas_call(finish, out_shape=jax.ShapeDtypeStruct((640, 4864), jnp.bf...  2.85 us

profile of v3, /device:TPU:0, one launch (start us, length us, event | category | flops | bytes accessed | tf_op | source)
XLA Modules:
  0.0 42.7 jit_solution(10965835200736629460)
XLA Ops:
  0.0 39.6 %shard_map.28 = (f32[640,4864]{1,0:T(8,128)S(1)}, f32[640,128]{1,0:T(8,128)S(1)}) custom-call(bf16[40,2048]{1,0:T(8,128)(2,1)} %x_hbm.1, bf16[2048,4864]{1,0:T(8,128)(2,1)} %w_hbm.1), custom_call_target="tpu_custom_call" | custom-call | flops 12750684160 | bytes 36000000 | tf_op jit(solution)/shard_map/pallas_call | solution.py:270
  39.6 2.9 %shard_map.29 = bf16[640,4864]{1,0:T(8,128)(2,1)} custom-call(f32[640,4864]{1,0:T(8,128)S(1)} %get-tuple-element.7.kept, f32[640,128]{1,0:T(8,128)S(1)} %get-tuple-element.8.scale), custom_call_target="tpu_custom_call" | custom-call | flops 3112960 | bytes 19000000 | tf_op jit(solution)/shard_map/pallas_call | solution.py:298

commit v4 on v3

--- a/solution.py
+++ b/solution.py
@@ -198,6 +198,9 @@
     def exchanged(step):
         pltpu.make_async_copy(row_recv.at[step], row_recv.at[step], row_recv_sem.at[step]).wait()
 
+    def sent(step):
+        pltpu.make_async_copy(row_recv.at[step], row_recv.at[step], row_send_sem.at[step]).wait()
+
     tiles = [slice(i * 128, (i + 1) * 128) for i in range(5)]
     for t in tiles:
         row_send[0, :, t] = jnp.max(to_row(lane[t, :]), axis=0, keepdims=True)
@@ -214,18 +217,21 @@
             kept[r, c:c + 128] = ratio
             square[r, c:c + 128] = ratio * ratio
 
+    for copy in started:
+        copy.wait_send()
     exchanged(0)
+    sent(0)
     local = row_send[0]
     peak = jnp.maximum(local, jnp.max(row_recv[0], axis=0))
     shrink = jnp.exp(local - peak)
     for t in tiles:
         peak_col[t, :] = to_column(shrink[:, t] * 20.0)
 
-    @pl.loop(0, 20)
+    @pl.loop(0, 10)
     def _(i):
-        r = pl.ds(pl.multiple_of(i * 32, 32), 32)
+        r = pl.ds(pl.multiple_of(i * 64, 64), 64)
         factor = peak_col[r, :]
-        total = jnp.zeros((32, 128), F32)
+        total = jnp.zeros((64, 128), F32)
         for c in range(0, 4864, 128):
             ratio = kept[r, c:c + 128]
             value = jnp.minimum(jnp.maximum(square[r, c:c + 128] * factor - ratio, 0.0), ratio)
@@ -238,23 +244,19 @@
     exchange(1)
     exchanged(1)
     mass = row_send[1] + jnp.sum(row_recv[1], axis=0)
-    final = shrink / mass
-    for t in tiles:
-        scale[t, :] = to_column(final[:, t])
-
-    for copy in started:
-        copy.wait_send()
-    for step in range(2):
-        pltpu.make_async_copy(row_recv.at[step], row_recv.at[step], row_send_sem.at[step]).wait()
-
-
-def finish(kept, scale, out, stage, sem):
+    scale[...] = shrink / mass
+
+    sent(1)
+
+
+def finish(kept, scale, out, column, stage, sem):
     copies = []
     for i in range(20):
-        @pl.loop(0, 2)
-        def _(j):
-            r = pl.ds(pl.multiple_of(i * 32 + j * 16, 16), 16)
-            factor = scale[r, :]
+        if i % 4 == 0:
+            column[...] = to_column(scale[:, i * 32:i * 32 + 128])
+        for j in range(0, 32, 16):
+            r = slice(i * 32 + j, i * 32 + j + 16)
+            factor = column[i % 4 * 32 + j:i % 4 * 32 + j + 16, :]
             for c in range(0, 4864, 128):
                 stage[r, c:c + 128] = (kept[r, c:c + 128] * factor).astype(jnp.bfloat16)
         rows = pl.ds(i * 32, 32)
@@ -269,7 +271,7 @@
     hidden_rows = pltpu.with_memory_space_constraint(hidden_rows, pltpu.HBM)
     kept, scale = pl.pallas_call(
         kernel,
-        out_shape=(pltpu.VMEM((640, 4864), F32), pltpu.VMEM((640, 128), F32)),
+        out_shape=(pltpu.VMEM((640, 4864), F32), pltpu.VMEM((1, 640), F32)),
         in_specs=[pl.BlockSpec(memory_space=pltpu.HBM)] * 2,
         out_specs=(pl.BlockSpec(memory_space=pltpu.VMEM),) * 2,
         scratch_shapes=[
@@ -300,7 +302,11 @@
         out_shape=jax.ShapeDtypeStruct((640, 4864), jnp.bfloat16),
         in_specs=[pl.BlockSpec(memory_space=pltpu.VMEM)] * 2,
         out_specs=pl.BlockSpec(memory_space=pl.ANY),
-        scratch_shapes=[pltpu.VMEM((640, 4864), jnp.bfloat16), pltpu.SemaphoreType.DMA((20,))],
+        scratch_shapes=[
+            pltpu.VMEM((128, 128), F32),
+            pltpu.VMEM((640, 4864), jnp.bfloat16),
+            pltpu.SemaphoreType.DMA((20,)),
+        ],
         compiler_params=pltpu.CompilerParams(vmem_limit_bytes=10 * 2**20),
         cost_estimate=pl.CostEstimate(flops=640 * 4864, bytes_accessed=19 * 10**6, transcendentals=0),
     )(kept, scale)

time: 42.8 us -> 42.6 us (level)
  no operation moved by 1% of the time
where the time goes in v4:
time: 42.6 us; the launch traced here: 42.5 us
  Pallas kernels  42.4 us (100%)
    pallas_call x1, Pallas kernels, body(): pl.pallas_call(kernel, out_shape=(pltpu.VMEM((640, 4864), F32), pltpu.VME...  39.4 us
    pallas_call x1, Pallas kernels, body(): pl.pallas_call(finish, out_shape=jax.ShapeDtypeStruct((640, 4864), jnp.bf...  2.91 us

profile of v4, /device:TPU:0, one launch (start us, length us, event | category | flops | bytes accessed | tf_op | source)
XLA Modules:
  0.0 42.5 jit_solution(17045342711527639887)
XLA Ops:
  0.0 39.4 %shard_map.28 = (f32[640,4864]{1,0:T(8,128)S(1)}, f32[1,640]{1,0:T(1,128)S(1)}) custom-call(bf16[40,2048]{1,0:T(8,128)(2,1)} %x_hbm.1, bf16[2048,4864]{1,0:T(8,128)(2,1)} %w_hbm.1), custom_call_target="tpu_custom_call" | custom-call | flops 12750684160 | bytes 36000000 | tf_op jit(solution)/shard_map/pallas_call | solution.py:272
  39.5 2.9 %shard_map.29 = bf16[640,4864]{1,0:T(8,128)(2,1)} custom-call(f32[640,4864]{1,0:T(8,128)S(1)} %get-tuple-element.7.kept, f32[1,640]{1,0:T(1,128)S(1)} %get-tuple-element.8.scale), custom_call_target="tpu_custom_call" | custom-call | flops 3112960 | bytes 19000000 | tf_op jit(solution)/shard_map/pallas_call | solution.py:300
